TPU v7x, 32 devices: a whole 2x2x4 slice. The times are simulated.
32 devices in a mesh: gy: 2 (over x), gx: 4 (over z), gz: 4 (over y, core).
Axes of the slice: x: 2, y: 2, z: 4, core: 2. Of those that a mesh axis runs over, the one named last changes fastest.
Arguments:
- adjoint: float32 [3, 64, 256, 512], P(None, 'gx', 'gy', 'gz'), may hold values from -6 to 6
- base_flow: float32 [3, 64, 256, 512], P(None, 'gx', 'gy', 'gz'), may hold values from -4 to 4
- viscosity: float32 [64, 256, 512], P('gx', 'gy', 'gz'), may hold values from 0.3 to 3
- first_matrix: float32 [256, 256], replicated, may hold values from -0.375 to 0.375
- second_matrix: float32 [256, 256], replicated, may hold values from -0.375 to 0.375
Outputs:
- earlier: float32 [3, 64, 256, 512], P(None, 'gx', 'gy', 'gz')
All inputs are finite; a program needn't handle non-finite values.
Results may differ from a plain program's by a relative error of at most 0.00012.
Values sent between devices are 32-bit elements; how exact they have to be, the bound alone decides.
A program may use at most 128 MiB of HBM per device.

v0:
```python
import jax
import jax.numpy as jnp
from jax import lax
from jax.sharding import PartitionSpec as P

STEPS = 2


advect_scale = 0.25
diffuse_scale = 0.1


def with_halo(shard, sides, width):
    for axis, dim in sides:
        count, length = (lax.axis_size(axis), shard.shape[dim])
        up = [(i, (i + 1) % count) for i in range(count)]
        down = [(j, i) for i, j in up]
        last = lax.slice_in_dim(shard, length - width, length, axis=dim)
        initial = lax.slice_in_dim(shard, 0, width, axis=dim)
        before = lax.ppermute(last, axis, up)
        after = lax.ppermute(initial, axis, down)
        shard = jnp.concatenate([before, shard, after], axis=dim)
    return shard


def normal_derivs(extended, matrices):
    local_rows = extended.shape[2]
    owned = lax.dynamic_slice_in_dim(matrices, lax.axis_index("gy") * local_rows, local_rows, 1)
    return jnp.einsum(
        "kij,cxjz->kcxiz",
        owned,
        lax.all_gather(extended, "gy", axis=2, tiled=True),
        precision=lax.Precision.HIGHEST,
    )


def advance_state(extended, velocity, kinematic, visc_slope, matrices):
    derived = normal_derivs(extended, matrices)
    stream_cells = extended.shape[1] - 4
    span_cells = extended.shape[3] - 4

    def offset_view(values, along_x, along_z):
        return values[
            :, 2 + along_x : 2 + along_x + stream_cells, :, 2 + along_z : 2 + along_z + span_cells
        ]

    current = offset_view(extended, 0, 0)
    east = offset_view(extended, 1, 0)
    west = offset_view(extended, -1, 0)
    stream_slope = (
        8.0 * (east - west) - (offset_view(extended, 2, 0) - offset_view(extended, -2, 0))
    ) / 12.0
    upper = offset_view(extended, 0, 1)
    lower = offset_view(extended, 0, -1)
    span_slope = (
        8.0 * (upper - lower) - (offset_view(extended, 0, 2) - offset_view(extended, 0, -2))
    ) / 12.0
    centre_visc = offset_view(kinematic, 0, 0)
    stream_flux = 0.5 * (centre_visc + offset_view(kinematic, 1, 0)) * (east - current) - 0.5 * (
        offset_view(kinematic, -1, 0) + centre_visc
    ) * (current - west)
    span_flux = 0.5 * (centre_visc + offset_view(kinematic, 0, 1)) * (upper - current) - 0.5 * (
        offset_view(kinematic, 0, -1) + centre_visc
    ) * (current - lower)
    normal_first = offset_view(derived[0], 0, 0)
    normal_second = offset_view(derived[1], 0, 0)
    speeds = offset_view(velocity, 0, 0)
    updated = (
        current
        + advect_scale
        * (speeds[0:1] * stream_slope + speeds[1:2] * normal_first + speeds[2:3] * span_slope)
        + diffuse_scale
        * (
            stream_flux
            + span_flux
            + centre_visc * normal_second
            + offset_view(visc_slope, 0, 0) * normal_first
        )
    )
    local_rows = extended.shape[2]
    global_rows = lax.axis_index("gy") * local_rows + jnp.arange(local_rows, dtype=jnp.int32)
    total_rows = local_rows * lax.axis_size("gy")
    wall_mask = (
        ((global_rows > 0) & (global_rows < total_rows - 1))
        .astype(jnp.float32)
        .reshape(1, 1, local_rows, 1)
    )
    return updated * wall_mask


def per_device(adjoint, base_flow, viscosity, first_matrix, second_matrix):
    outer = 2
    matrices = jnp.stack([first_matrix, second_matrix])
    combined = jnp.concatenate([base_flow, viscosity[None]], 0)
    padded = with_halo(combined, (("gx", 1), ("gz", 3)), outer)
    velocity = padded[0:3]
    kinematic = padded[3:4]
    local_rows = kinematic.shape[2]
    first_owned = lax.dynamic_slice_in_dim(
        first_matrix, lax.axis_index("gy") * local_rows, local_rows, 0
    )
    visc_slope = jnp.einsum(
        "ij,cxjz->cxiz",
        first_owned,
        lax.all_gather(kinematic, "gy", axis=2, tiled=True),
        precision=lax.Precision.HIGHEST,
    )
    current = adjoint
    for step_index in range(STEPS):
        extended = with_halo(current, (("gx", 1), ("gz", 3)), 2)
        current = advance_state(extended, velocity, kinematic, visc_slope, matrices)
    return current


def solution(mesh):
    return jax.shard_map(
        per_device,
        mesh=mesh,
        in_specs=(
            P(None, "gx", "gy", "gz"),
            P(None, "gx", "gy", "gz"),
            P("gx", "gy", "gz"),
            P(),
            P(),
        ),
        out_specs=P(None, "gx", "gy", "gz"),
        check_vma=False,
    )
```

profile of v0, /device:TPU:3, one launch (start us, length us, event | category | flops | bytes accessed | tf_op | source)
XLA Modules:
  0.0 387.9 jit_solution(16616714666613950659)
XLA Ops:
  6.5 2.6 copy.16
  9.1 2.4 copy.17
  16.4 11.4 %collective-permute-done.5 = f32[4,2,128,128]{2,3,1,0:T(8,128)S(1)} collective-permute-done((f32[4,2,128,128]{2,3,1,0:T(8,128)S(1)}, f32[4,2,128,128]{2,3,1,0:T(8,128)S(1)}, u32[]{:S(2)}, u32[]{:S(2)}) %collective-permute-start.5) | collective-permute-done | bytes 524320 | tf_op jit(solution)/shard_map/ppermute | solution.py:20
  27.8 11.0 %collective-permute-done.4 = f32[4,2,128,128]{2,3,1,0:T(8,128)S(1)} collective-permute-done((f32[4,2,128,128]{2,3,1,0:T(8,128)S(1)}, f32[4,2,128,128]{2,3,1,0:T(8,128)S(1)}, u32[]{:S(2)}, u32[]{:S(2)}) %collective-permute-start.4) | collective-permute-done | bytes 524320 | tf_op jit(solution)/shard_map/ppermute | solution.py:21
  42.6 2.4 collective-permute-done.6
  46.9 2.4 copy.15
  50.3 2.4 collective-permute-start
  52.7 9.6 %collective-permute-done.1 = f32[3,2,128,128]{2,3,1,0:T(8,128)S(1)} collective-permute-done((f32[3,2,128,128]{2,3,1,0:T(8,128)S(1)}, f32[3,2,128,128]{2,3,1,0:T(8,128)S(1)}, u32[]{:S(2)}, u32[]{:S(2)}) %collective-permute-start.1) | collective-permute-done | bytes 393248 | tf_op jit(solution)/shard_map/ppermute | solution.py:20
  62.3 7.4 %collective-permute-done = f32[3,2,128,128]{2,3,1,0:T(8,128)S(1)} collective-permute-done((f32[3,2,128,128]{2,3,1,0:T(8,128)S(1)}, f32[3,2,128,128]{2,3,1,0:T(8,128)S(1)}, u32[]{:S(2)}, u32[]{:S(2)}) %collective-permute-start) | collective-permute-done | bytes 393248 | tf_op jit(solution)/shard_map/ppermute | solution.py:21
  71.9 2.8 collective-permute-done.3
  75.3 2.6 pad_maximum_fusion
  78.2 3.6 multiply_bitcast_fusion.1
  81.8 2.5 copy.10
  84.3 2.5 copy.11
  86.8 2.6 copy.14
  89.4 5.1 %pad_maximum_fusion.1 = (f32[3,20,128,130]{2,3,1,0:T(8,128)}, f32[3,20,128,130]{2,3,1,0:T(8,128)}) fusion(f32[3,20,128,2]{2,3,1,0:T(2,128)} %copy-done.18, f32[3,2,128,128]{2,3,1,0:T(8,128)} %copy-done.5, f32[3,16,128,128]{2,3,1,0:T(8,128)S(1)} %copy.15, f32[3,2,128,128]{2,3,1,0:T(8,128)S(1)} %collective-permute-done.1, f32[3,20,128,2]{2,3,1,0:T(2,128)} %copy-done.17), kind=kLoop, calls=%fused_computation.9 | loop fusion | flops 5990400 | bytes 12042240 | tf_op jit(solution)/shard_map/concatenate | solution.py:22
  94.6 2.3 fusion.52
  96.9 4.8 %fusion.44 = f32[1,20,128,132]{2,3,1,0:T(8,128)S(1)} fusion(f32[1,20,256,132]{2,3,1,0:T(8,128)} %all-gather.6.cloned.1.call-done, f32[256,256]{1,0:T(8,128)S(1)} %copy-done.11, s32[]{:T(128)S(6)} %select_n.2), kind=kOutput, calls=%fused_computation.66 | convolution fusion | flops 1038090240 | bytes 4186116 | tf_op jit(solution)/shard_map/ij,cxjz->cxiz/dot_general | solution.py:102
  102.9 88.1 %all-gather.4.cloned.1.call-done = f32[3,20,256,132]{2,3,1,0:T(8,128)} async-done(((f32[3,20,128,132]{2,3,1,0:T(8,128)}), f32[3,20,256,132]{2,3,1,0:T(8,128)}) %all-gather.4.cloned.1.call-update) | async-done | bytes 8110096 | tf_op jit(solution)/shard_map/all_gather | solution.py:32
  190.9 9.5 %fusion.4 = f32[2,3,20,128,132]{3,4,2,1,0:T(8,128)S(1)} fusion(f32[3,20,256,132]{2,3,1,0:T(8,128)} %all-gather.4.cloned.1.call-done, s32[]{:T(128)S(6)} %select_n.2, f32[1,256,256]{2,1,0:T(8,128)S(1)} %bitcast.64, f32[1,256,256]{2,1,0:T(8,128)S(1)} %bitcast.66), kind=kOutput, calls=%fused_computation.22 | convolution fusion | flops 6228606976 | bytes 16744452 | tf_op jit(solution)/shard_map/kij,cxjz->kcxiz/dot_general | solution.py:29
  200.5 3.8 slice_bitcast_fusion.3
  204.3 16.3 %fusion.32 = f32[3,16,128,128]{2,3,1,0:T(8,128)S(1)} fusion(f32[3,20,128,132]{2,3,1,0:T(8,128)} %get-tuple-element.8, f32[3,16,128,128]{2,3,1,0:T(8,128)} %copy-done, f32[3,20,128,130]{2,3,1,0:T(8,128)} %get-tuple-element.22, f32[3,20,128,130]{2,3,1,0:T(8,128)} %get-tuple-element.21, f32[3,2,128,128]{2,3,1,0:T(8,128)S(1)} %collective-permute-done.1, ...), kind=kLoop, calls=%fused_computation.51 | loop fusion | flops 29097984 | bytes 35389952 | tf_op jit(solution)/shard_map/mul | solution.py:88
  224.0 8.7 %collective-permute-done.9 = f32[3,2,128,128]{2,3,1,0:T(8,128)S(1)} collective-permute-done((f32[3,2,128,128]{2,3,1,0:T(8,128)S(1)}, f32[3,2,128,128]{2,3,1,0:T(8,128)S(1)}, u32[]{:S(2)}, u32[]{:S(2)}) %collective-permute-start.9) | collective-permute-done | bytes 393248 | tf_op jit(solution)/shard_map/ppermute | solution.py:20
  232.8 8.2 %collective-permute-done.8 = f32[3,2,128,128]{2,3,1,0:T(8,128)S(1)} collective-permute-done((f32[3,2,128,128]{2,3,1,0:T(8,128)S(1)}, f32[3,2,128,128]{2,3,1,0:T(8,128)S(1)}, u32[]{:S(2)}, u32[]{:S(2)}) %collective-permute-start.8) | collective-permute-done | bytes 393248 | tf_op jit(solution)/shard_map/ppermute | solution.py:21
  244.5 2.4 collective-permute-done.11
  247.5 2.6 pad_maximum_fusion.2
  250.0 5.0 %pad_maximum_fusion.3 = (f32[3,20,128,130]{2,3,1,0:T(8,128)}, f32[3,20,128,130]{2,3,1,0:T(8,128)}) fusion(f32[3,20,128,2]{2,3,1,0:T(2,128)} %copy-done.20, f32[3,2,128,128]{2,3,1,0:T(8,128)} %copy-done.6, f32[3,16,128,128]{2,3,1,0:T(8,128)S(1)} %fusion.32, f32[3,2,128,128]{2,3,1,0:T(8,128)S(1)} %collective-permute-done.9, f32[3,20,128,2]{2,3,1,0:T(2,128)} %copy-done.19), kind=kLoop, calls=%fused_computation.12 | loop fusion | flops 5990400 | bytes 12042240 | tf_op jit(solution)/shard_map/concatenate | solution.py:22
  255.0 96.4 %all-gather.8.cloned.1.call-done = f32[3,20,256,132]{2,3,1,0:T(8,128)} async-done(((f32[3,20,128,132]{2,3,1,0:T(8,128)}), f32[3,20,256,132]{2,3,1,0:T(8,128)}) %all-gather.8.cloned.1.call-update) | async-done | bytes 8110096 | tf_op jit(solution)/shard_map/all_gather | solution.py:32
  351.4 9.6 %fusion.7 = f32[2,3,20,128,132]{3,4,2,1,0:T(8,128)S(1)} fusion(f32[3,20,256,132]{2,3,1,0:T(8,128)} %all-gather.8.cloned.1.call-done, s32[]{:T(128)S(6)} %select_n.2, f32[1,256,256]{2,1,0:T(8,128)} %bitcast.63, f32[1,256,256]{2,1,0:T(8,128)} %bitcast.65), kind=kOutput, calls=%fused_computation.23 | convolution fusion | flops 6228606976 | bytes 16744452 | tf_op jit(solution)/shard_map/kij,cxjz->kcxiz/dot_general | solution.py:29
  361.0 3.8 slice_bitcast_fusion.1
  364.8 13.0 %fusion.18 = f32[3,16,128,128]{2,3,1,0:T(8,128)} fusion(f32[3,20,128,132]{2,3,1,0:T(8,128)} %get-tuple-element.6, f32[3,16,128,128]{2,3,1,0:T(8,128)S(1)} %fusion.32, f32[3,20,128,130]{2,3,1,0:T(8,128)} %get-tuple-element.18, f32[3,20,128,130]{2,3,1,0:T(8,128)} %get-tuple-element.17, f32[3,2,128,128]{2,3,1,0:T(8,128)S(1)} %collective-permute-done.9, ...), kind=kLoop, calls=%fused_computation.33 | loop fusion | flops 29097984 | bytes 35389952 | tf_op jit(solution)/shard_map/mul | solution.py:88
  377.8 3.6 copy.24
  (72 shorter events, 23.3 us)
Async XLA Ops:
  6.5 90.4 %all-gather.6.cloned.1.call-start = ((), (), s32[]{:S(2)}) async-start(), calls=%async_computation.1 | async-start | bytes 4177920 | tf_op jit(solution)/shard_map/all_gather | solution.py:105
  11.5 33.5 %copy-start.1 = (f32[3,16,128,128]{2,3,1,0:T(8,128)}, f32[3,16,128,128]{2,3,1,0:T(8,128)S(1)}, u32[]{:S(2)}) copy-start(f32[3,16,128,128]{2,3,1,0:T(8,128)S(1)} %copy.17) | copy-start | bytes 9437188
  11.5 27.3 %copy-start.3 = (f32[16,128,128]{1,2,0:T(8,128)S(1)}, f32[16,128,128]{1,2,0:T(8,128)}, u32[]{:S(2)}) copy-start(f32[16,128,128]{1,2,0:T(8,128)} %copy.16) | copy-start | bytes 3145732
  13.0 14.8 %collective-permute-start.5 = (f32[4,2,128,128]{2,3,1,0:T(8,128)S(1)}, f32[4,2,128,128]{2,3,1,0:T(8,128)S(1)}, u32[]{:S(2)}, u32[]{:S(2)}) collective-permute-start(f32[4,2,128,128]{2,3,1,0:T(8,128)S(1)} %get-tuple-element.15), channel_id=1, source_target_pairs={{0,4},{4,8},{8,12},{12,0},{1,5},{5,9},{9,13},{13,1},{2,6},{6,10},{... | collective-permute-start | bytes 1572872 | tf_op jit(solution)/shard_map/ppermute | solution.py:20
  14.3 24.5 %collective-permute-start.4 = (f32[4,2,128,128]{2,3,1,0:T(8,128)S(1)}, f32[4,2,128,128]{2,3,1,0:T(8,128)S(1)}, u32[]{:S(2)}, u32[]{:S(2)}) collective-permute-start(f32[4,2,128,128]{2,3,1,0:T(8,128)S(1)} %get-tuple-element.16), channel_id=1, source_target_pairs={{4,0},{8,4},{12,8},{0,12},{5,1},{9,5},{13,9},{1,13},{6,2},{10,6},{... | collective-permute-start | bytes 1572872 | tf_op jit(solution)/shard_map/ppermute | solution.py:21
  27.8 17.2 %copy-start.7 = (f32[4,2,128,128]{2,3,1,0:T(8,128)}, f32[4,2,128,128]{2,3,1,0:T(8,128)S(1)}, u32[]{:S(2)}) copy-start(f32[4,2,128,128]{2,3,1,0:T(8,128)S(1)} %collective-permute-done.5) | copy-start | bytes 1572868
  38.8 6.2 %copy-start.9 = (f32[4,2,128,128]{2,3,1,0:T(8,128)}, f32[4,2,128,128]{2,3,1,0:T(8,128)S(1)}, u32[]{:S(2)}) copy-start(f32[4,2,128,128]{2,3,1,0:T(8,128)S(1)} %collective-permute-done.4) | copy-start | bytes 1572868
  38.8 3.8 collective-permute-start.7
  41.1 3.9 collective-permute-start.6
  42.6 2.4 copy-start.13
  46.9 144.0 %all-gather.4.cloned.1.call-start = ((), (), s32[]{:S(2)}) async-start(), calls=%async_computation | async-start | bytes 12533760 | tf_op jit(solution)/shard_map/all_gather | solution.py:32
  49.3 40.0 %copy-start = (f32[3,16,128,128]{2,3,1,0:T(8,128)}, f32[3,16,128,128]{2,3,1,0:T(8,128)S(1)}, u32[]{:S(2)}) copy-start(f32[3,16,128,128]{2,3,1,0:T(8,128)S(1)} %copy.15) | copy-start | bytes 9437188
  49.4 12.9 %collective-permute-start.1 = (f32[3,2,128,128]{2,3,1,0:T(8,128)S(1)}, f32[3,2,128,128]{2,3,1,0:T(8,128)S(1)}, u32[]{:S(2)}, u32[]{:S(2)}) collective-permute-start(f32[3,2,128,128]{2,3,1,0:T(8,128)S(1)} %get-tuple-element.30), channel_id=1, source_target_pairs={{0,4},{4,8},{8,12},{12,0},{1,5},{5,9},{9,13},{13,1},{2,6},{6,10},{... | collective-permute-start | bytes 1179656 | tf_op jit(solution)/shard_map/ppermute | solution.py:20
  50.3 19.4 %collective-permute-start = (f32[3,2,128,128]{2,3,1,0:T(8,128)S(1)}, f32[3,2,128,128]{2,3,1,0:T(8,128)S(1)}, u32[]{:S(2)}, u32[]{:S(2)}) collective-permute-start(f32[3,2,128,128]{2,3,1,0:T(8,128)S(1)} %get-tuple-element.31), channel_id=1, source_target_pairs={{4,0},{8,4},{12,8},{0,12},{5,1},{9,5},{13,9},{1,13},{6,2},{10,6},{... | collective-permute-start | bytes 1179656 | tf_op jit(solution)/shard_map/ppermute | solution.py:21
  69.8 4.8 %copy-start.5 = (f32[3,2,128,128]{2,3,1,0:T(8,128)}, f32[3,2,128,128]{2,3,1,0:T(8,128)S(1)}, u32[]{:S(2)}) copy-start(f32[3,2,128,128]{2,3,1,0:T(8,128)S(1)} %collective-permute-done) | copy-start | bytes 1179652
  69.8 2.0 collective-permute-start.2
  70.6 4.0 %collective-permute-start.3 = (f32[3,20,128,2]{2,3,1,0:T(2,128)S(1)}, f32[3,20,128,2]{2,3,1,0:T(2,128)S(1)}, u32[]{:S(2)}, u32[]{:S(2)}) collective-permute-start(f32[3,20,128,2]{2,3,1,0:T(2,128)S(1)} %get-tuple-element.24), channel_id=1, source_target_pairs={{1,0},{2,1},{3,2},{0,3},{5,4},{6,5},{7,6},{4,7},{9,8},{10,9},{11,1... | collective-permute-start | bytes 184328 | tf_op jit(solution)/shard_map/ppermute | solution.py:21
  71.9 2.8 copy-start.17
  77.9 273.5 %all-gather.8.cloned.1.call-start = ((), (), s32[]{:S(2)}) async-start(), calls=%async_computation.2 | async-start | bytes 12533760 | tf_op jit(solution)/shard_map/all_gather | solution.py:32
  89.4 5.2 %copy-start.2 = (f32[3,16,128,128]{2,3,1,0:T(8,128)S(1)}, f32[3,16,128,128]{2,3,1,0:T(8,128)}, u32[]{:S(2)}) copy-start(f32[3,16,128,128]{2,3,1,0:T(8,128)} %copy-done.1) | copy-start | bytes 9437188
  89.4 5.2 %copy-start.4 = (f32[16,128,128]{1,2,0:T(8,128)S(1)}, f32[16,128,128]{1,2,0:T(8,128)}, u32[]{:S(2)}) copy-start(f32[16,128,128]{1,2,0:T(8,128)} %copy.16) | copy-start | bytes 3145732
  89.4 5.2 %copy-start.8 = (f32[4,2,128,128]{2,3,1,0:T(8,128)S(1)}, f32[4,2,128,128]{2,3,1,0:T(8,128)}, u32[]{:S(2)}) copy-start(f32[4,2,128,128]{2,3,1,0:T(8,128)} %copy-done.7) | copy-start | bytes 1572868
  89.4 5.2 %copy-start.10 = (f32[4,2,128,128]{2,3,1,0:T(8,128)S(1)}, f32[4,2,128,128]{2,3,1,0:T(8,128)}, u32[]{:S(2)}) copy-start(f32[4,2,128,128]{2,3,1,0:T(8,128)} %copy-done.9) | copy-start | bytes 1572868
  89.4 5.2 %copy-start.14 = (f32[4,20,128,2]{2,3,1,0:T(2,128)S(1)}, f32[4,20,128,2]{2,3,1,0:T(2,128)}, u32[]{:S(2)}) copy-start(f32[4,20,128,2]{2,3,1,0:T(2,128)} %copy-done.13) | copy-start | bytes 245764
  89.4 5.2 %copy-start.16 = (f32[4,20,128,2]{2,3,1,0:T(2,128)S(1)}, f32[4,20,128,2]{2,3,1,0:T(2,128)}, u32[]{:S(2)}) copy-start(f32[4,20,128,2]{2,3,1,0:T(2,128)} %copy-done.15) | copy-start | bytes 245764
  96.9 94.0 %copy-start.12 = (f32[256,256]{1,0:T(8,128)S(1)}, f32[256,256]{1,0:T(8,128)}, u32[]{:S(2)}) copy-start(f32[256,256]{1,0:T(8,128)} %param.9) | copy-start | bytes 786436
  220.7 12.1 %collective-permute-start.9 = (f32[3,2,128,128]{2,3,1,0:T(8,128)S(1)}, f32[3,2,128,128]{2,3,1,0:T(8,128)S(1)}, u32[]{:S(2)}, u32[]{:S(2)}) collective-permute-start(f32[3,2,128,128]{2,3,1,0:T(8,128)S(1)} %get-tuple-element.25), channel_id=1, source_target_pairs={{0,4},{4,8},{8,12},{12,0},{1,5},{5,9},{9,13},{13,1},{2,6},{6,10},{... | collective-permute-start | bytes 1179656 | tf_op jit(solution)/shard_map/ppermute | solution.py:20
  222.0 18.9 %collective-permute-start.8 = (f32[3,2,128,128]{2,3,1,0:T(8,128)S(1)}, f32[3,2,128,128]{2,3,1,0:T(8,128)S(1)}, u32[]{:S(2)}, u32[]{:S(2)}) collective-permute-start(f32[3,2,128,128]{2,3,1,0:T(8,128)S(1)} %get-tuple-element.26), channel_id=1, source_target_pairs={{4,0},{8,4},{12,8},{0,12},{5,1},{9,5},{13,9},{1,13},{6,2},{10,6},{... | collective-permute-start | bytes 1179656 | tf_op jit(solution)/shard_map/ppermute | solution.py:21
  240.9 5.9 %copy-start.6 = (f32[3,2,128,128]{2,3,1,0:T(8,128)}, f32[3,2,128,128]{2,3,1,0:T(8,128)S(1)}, u32[]{:S(2)}) copy-start(f32[3,2,128,128]{2,3,1,0:T(8,128)S(1)} %collective-permute-done.8) | copy-start | bytes 1179652
  241.0 3.5 collective-permute-start.10
  243.2 3.6 collective-permute-start.11
  244.5 2.4 copy-start.19
  (4 other events, 4.2 us)
Sparse Core Ops, SparseCore 0:
  47.0 38.6 all-gather.5
  87.3 103.5 all-gather.3
  250.2 101.1 all-gather.7
where the time goes:
time: 391 us; the launch traced here: 388 us
  waiting for transfers between devices  252 us (64%)
  other arithmetic  53.3 us (14%)
  local copies, waits for them, and re-layouts  29.4 us (8%)
  matrix products  23.9 us (6%)
  starting transfers between devices  15.6 us (4%)
  between operations  13.4 us (3%)
    all_gather x2, waiting for transfers between devices, normal_derivs(): lax.all_gather(extended, 'gy', axis=2, tiled=True)  184 us
    ppermute x6, waiting for transfers between devices, with_halo(): after = lax.ppermute(initial, axis, down)  34.1 us
    ppermute x6, waiting for transfers between devices, with_halo(): before = lax.ppermute(last, axis, up)  33.8 us
    mul x2, other arithmetic, advance_state(): return updated * wall_mask  29.3 us
    dot_general x2, matrix products, normal_derivs(): jnp.einsum('kij,cxjz->kcxiz', owned, lax.all_gather(extended, 'gy', axis=...  19.1 us
    concatenate x6, other arithmetic, with_halo(): shard = jnp.concatenate([before, shard, after], axis=dim)  16.5 us
    unnamed x45, local copies, waits for them, and re-layouts  9.32 us
    ppermute x6, starting transfers between devices, with_halo(): before = lax.ppermute(last, axis, up)  8.82 us
  transfers between devices with their start and end apart: 15, of which 14 were waited for; matrix products, arithmetic and copies ran while one was open for 9% of the time, Pallas kernels for 0%

commit v1 on v0

v1 whole, which is shorter than its diff:
```python
import jax
import jax.numpy as jnp
from jax import lax
from jax.experimental import pallas as pl
from jax.experimental.pallas import tpu as pltpu
from jax.sharding import PartitionSpec as P

STEPS = 2
MESH = pl.DeviceIdType.MESH
F32 = jnp.float32
BF16 = jnp.bfloat16


def kernel(
    adj, flow, visc, first_m, second_m, out,
    send, state, mid, coef, late, back, matrix, rhs, derived,
    edge_out, edges, outer, rim_lo, rim_hi, edges1, inner1, outer1,
    swap_s, swap_r, edge_s, edge_r, rim_s, rim_r, ret_s, ret_r,
):
    _, cells, half_rows, lanes = adj.shape
    rows = 2 * half_rows
    half = lanes // 2
    pairs = cells // 2
    chunk = 32
    ngx, ngz = lax.axis_size("gx"), lax.axis_size("gz")
    gy, gx, gz = lax.axis_index("gy"), lax.axis_index("gx"), lax.axis_index("gz")
    upper = lax.rem(gy + gz, 2)
    peer = (1 - gy, gx, gz)
    left = (gy, lax.rem(gx + ngx - 1, ngx), gz)
    right = (gy, lax.rem(gx + 1, ngx), gz)
    beside = (gy, gx, lax.rem(gz + ngz - 1 + 2 * upper, ngz))
    mine = pl.ds(pl.multiple_of(gy * half_rows, half_rows), half_rows)
    other = pl.ds(pl.multiple_of((1 - gy) * half_rows, half_rows), half_rows)

    def remote(src, dst, s, r, device):
        return pltpu.make_async_remote_copy(
            src_ref=src, dst_ref=dst, send_sem=s, recv_sem=r, device_id=device, device_id_type=MESH
        )

    def swap(p):
        return remote(send.at[p], state.at[p + 1, :, mine, :], swap_s.at[p], swap_r.at[p], peer)

    def give_back(p):
        return remote(late.at[p, :, other, :], back.at[p], ret_s.at[p], ret_r.at[p], peer)

    swap_edges = remote(edge_out, edges.at[:, mine, :], edge_s.at[0], edge_r.at[0], peer)
    pass_edge = remote(edges.at[1], outer, edge_s.at[1], edge_r.at[1], beside)
    swap_inner1 = remote(edges1.at[0], inner1, edge_s.at[2], edge_r.at[2], peer)
    pass_outer1 = remote(edges1.at[1], outer1, edge_s.at[3], edge_r.at[3], beside)
    rim_left0 = remote(
        state.at[1, 0:4], state.at[pairs + 1, 0:4], rim_s.at[0], rim_r.at[0], left
    )
    rim_right0 = remote(state.at[pairs, 0:4], state.at[0, 0:4], rim_s.at[1], rim_r.at[1], right)
    rim_left1 = remote(mid.at[1], mid.at[pairs + 1], rim_s.at[2], rim_r.at[2], left)
    rim_right1 = remote(mid.at[pairs], mid.at[0], rim_s.at[3], rim_r.at[3], right)

    barrier = pltpu.get_barrier_semaphore()
    for device in (peer, left, right, beside):
        pl.semaphore_signal(barrier, inc=1, device_id=device, device_id_type=MESH)
    pl.semaphore_wait(barrier, 4)

    lane = lax.broadcasted_iota(jnp.int32, (half_rows, lanes), 1)
    is_upper = jnp.full((half_rows, lanes), upper, jnp.int32) == 1
    in_slot = lax.rem(lane, half) // 2
    far = half + 2

    def turn(values, shift):
        return pltpu.roll(values, lax.rem(shift + 2 * lanes, lanes), 1)

    def pack(p):
        for f in range(7):
            if f < 3:
                even, odd = adj[f, 2 * p], adj[f, 2 * p + 1]
            elif f == 3:
                even, odd = visc[2 * p], visc[2 * p + 1]
            else:
                even, odd = flow[f - 4, 2 * p], flow[f - 4, 2 * p + 1]
            lows = jnp.where(lane < half, even, pltpu.roll(odd, half, 1))
            highs = jnp.where(lane < half, pltpu.roll(even, half, 1), odd)
            keep = jnp.where(is_upper, highs, lows)
            give = jnp.where(is_upper, lows, highs)
            state[p + 1, f, mine, :] = keep
            send[p, f] = give
            if f < 4:
                k = f * pairs + p
                slot = in_slot == k
                near_shift = 2 * k + far * upper
                far_shift = 2 * k + far * (1 - upper)
                edges[0, mine, :] = jnp.where(slot, turn(give, near_shift), edges[0, mine, :])
                edges[1, mine, :] = jnp.where(slot, turn(keep, near_shift), edges[1, mine, :])
                edge_out[0] = jnp.where(slot, turn(keep, far_shift), edge_out[0])
                edge_out[1] = jnp.where(slot, turn(give, far_shift), edge_out[1])

    zeros = jnp.zeros((half_rows, lanes), F32)
    for s in range(2):
        edges[s, mine, :] = zeros
        edge_out[s] = zeros
    pack(0)
    swap(0).start()

    @pl.loop(1, pairs)
    def _(i):
        p = pairs - i
        pack(p)

        @pl.when(i <= 1)
        def _():
            swap(p).start()

    swap_edges.start()
    swap(pairs - 2).start()

    @pl.loop(1, pairs - 2)
    def _(p):
        swap(p).start()

    for s, source in enumerate((first_m, second_m)):
        values = source[...]
        high = values.astype(BF16)
        low = (values - high.astype(F32)).astype(BF16)
        block = slice(s * rows, (s + 1) * rows)
        matrix[block, 0:rows] = high
        matrix[block, rows : 2 * rows] = high
        matrix[block, 2 * rows : 3 * rows] = low
    edges1[...] = jnp.zeros(edges1.shape, F32)

    def split(source, place, count):
        for c in range(count):
            values = source[place, c]
            high = values.astype(BF16)
            low = (values - high.astype(F32)).astype(BF16)
            columns = slice(c * lanes, (c + 1) * lanes)
            rhs[0:rows, columns] = high
            rhs[rows : 2 * rows, columns] = low
            rhs[2 * rows : 3 * rows, columns] = high
        width = count * lanes
        derived[:, 0:width] = jnp.dot(
            matrix[...], rhs[:, 0:width], preferred_element_type=F32
        )

    clane = lax.broadcasted_iota(jnp.int32, (chunk, lanes), 1)
    crow = lax.broadcasted_iota(jnp.int32, (chunk, lanes), 0)
    lower_lanes = clane < half
    in_half = lax.rem(clane, half)
    cslot = lax.rem(clane, half) // 2

    def join_rims(inner, outside):
        choose = jnp.full((rows, lanes), upper, jnp.int32) == 1
        rim_lo[...] = jnp.where(choose, inner, outside)
        rim_hi[...] = jnp.where(choose, outside, inner)

    def x_views(current, before, after):
        east = pltpu.roll(jnp.where(lower_lanes, after, current), half, 1)
        west = pltpu.roll(jnp.where(lower_lanes, current, before), half, 1)
        return east, west

    def z_rims(k, at):
        return turn(rim_lo[at, :], lanes - 2 - 2 * k), turn(rim_hi[at, :], half - 2 * k)

    def z_views(current, rims, step):
        under = jnp.where(in_half >= half - step, rims[0], current)
        over = jnp.where(in_half < step, rims[1], current)
        return pltpu.roll(under, step, 1), pltpu.roll(over, lanes - step, 1)

    def coefficients(p):
        @pl.loop(0, rows // chunk)
        def _(r):
            at = pl.ds(pl.multiple_of(r * chunk, chunk), chunk)
            centre = state[p + 1, 3, at, :]
            east, west = x_views(centre, state[p, 3, at, :], state[p + 2, 3, at, :])
            lower, above = z_views(centre, z_rims(3 * pairs + p, at), 1)
            ve, vw = 0.05 * (centre + east), 0.05 * (centre + west)
            vu, vl = 0.05 * (centre + above), 0.05 * (centre + lower)
            bx, by, bz = state[p + 1, 4, at, :], state[p + 1, 5, at, :], state[p + 1, 6, at, :]
            bx6, bz6 = bx * (1.0 / 6.0), bz * (1.0 / 6.0)
            coef[p, 0, at, :] = 1.0 - (ve + vw) - (vu + vl)
            coef[p, 1, at, :] = bx6 + ve
            coef[p, 2, at, :] = vw - bx6
            coef[p, 3, at, :] = bx * (1.0 / 48.0)
            coef[p, 4, at, :] = bz6 + vu
            coef[p, 5, at, :] = vl - bz6
            coef[p, 6, at, :] = bz * (1.0 / 48.0)
            coef[p, 7, at, :] = 0.25 * by + 0.1 * derived[at, 3 * lanes : 4 * lanes]
            coef[p, 8, at, :] = 0.1 * centre

    def advance(source, p, target, place, with_edges):
        @pl.loop(0, rows // chunk)
        def _(r):
            at = pl.ds(pl.multiple_of(r * chunk, chunk), chunk)
            at2 = pl.ds(pl.multiple_of(rows + r * chunk, chunk), chunk)
            row = crow + r * chunk
            inside = (row > 0) & (row < rows - 1)
            cs = [coef[p, n, at, :] for n in range(9)]
            for c in range(3):
                k = c * pairs + p
                current = source[p + 1, c, at, :]
                before, after = source[p, c, at, :], source[p + 2, c, at, :]
                east, west = x_views(current, before, after)
                rims = z_rims(k, at)
                lower, above = z_views(current, rims, 1)
                lower2, above2 = z_views(current, rims, 2)
                columns = slice(c * lanes, (c + 1) * lanes)
                value = (
                    cs[0] * current
                    + cs[1] * east
                    + cs[2] * west
                    + cs[3] * (before - after)
                    + cs[4] * above
                    + cs[5] * lower
                    + cs[6] * (lower2 - above2)
                    + cs[7] * derived[at, columns]
                    + cs[8] * derived[at2, columns]
                )
                value = jnp.where(inside, value, 0.0)
                target[place, c, at, :] = value
                if with_edges:
                    slot = cslot == k
                    edges1[0, at, :] = jnp.where(
                        slot, turn(value, 2 * k + far * (1 - upper)), edges1[0, at, :]
                    )
                    edges1[1, at, :] = jnp.where(
                        slot, turn(value, 2 * k + far * upper), edges1[1, at, :]
                    )

    swap(0).wait_recv()
    rim_left0.start()
    swap(pairs - 1).wait_recv()
    rim_right0.start()
    swap_edges.wait_recv()
    pass_edge.start()
    pass_edge.wait_recv()
    join_rims(edges[0], outer[...])

    @pl.loop(0, pairs)
    def _(i):
        p = jnp.where(i == 0, pairs - 1, i - 1)

        @pl.when(i == 0)
        def _():
            swap(pairs - 2).wait_recv()
            rim_left0.wait_recv()

        @pl.when(i == 1)
        def _():
            swap(1).wait_recv()
            rim_right0.wait_recv()

        @pl.when((i >= 2) & (i < pairs - 2))
        def _():
            swap(i).wait_recv()

        split(state, p + 1, 4)
        coefficients(p)
        advance(state, p, mid, p + 1, True)

        @pl.when(i == 0)
        def _():
            rim_right1.start()

        @pl.when(i == 1)
        def _():
            rim_left1.start()

    swap_inner1.start()
    pass_outer1.start()
    swap_inner1.wait_recv()
    pass_outer1.wait_recv()
    rim_left1.wait_recv()
    rim_right1.wait_recv()
    join_rims(inner1[...], outer1[...])

    @pl.loop(0, pairs)
    def _(p):
        split(mid, p + 1, 3)
        advance(mid, p, late, p, False)
        give_back(p).start()

    @pl.loop(0, pairs)
    def _(p):
        give_back(p).wait_recv()
        for c in range(3):
            keep = late[p, c, mine, :]
            got = back[p, c]
            lows = jnp.where(is_upper, got, keep)
            highs = jnp.where(is_upper, keep, got)
            out[c, 2 * p] = jnp.where(lane < half, lows, pltpu.roll(highs, half, 1))
            out[c, 2 * p + 1] = jnp.where(lane < half, pltpu.roll(lows, half, 1), highs)

    @pl.loop(0, pairs)
    def _(p):
        swap(p).wait_send()
        give_back(p).wait_send()

    for copy in (
        swap_edges, pass_edge, swap_inner1, pass_outer1,
        rim_left0, rim_right0, rim_left1, rim_right1,
    ):
        copy.wait_send()


def per_device(adjoint, base_flow, viscosity, first_matrix, second_matrix):
    _, cells, half_rows, lanes = adjoint.shape
    rows, pairs = 2 * half_rows, cells // 2
    plane = (rows, lanes)
    vmem = pl.BlockSpec(memory_space=pltpu.VMEM)
    dma = pltpu.SemaphoreType.DMA
    return pl.pallas_call(
        kernel,
        out_shape=jax.ShapeDtypeStruct(adjoint.shape, F32),
        in_specs=[vmem] * 5,
        out_specs=vmem,
        scratch_shapes=[
            pltpu.VMEM((pairs, 7, half_rows, lanes), F32),
            pltpu.VMEM((pairs + 2, 7) + plane, F32),
            pltpu.VMEM((pairs + 2, 3) + plane, F32),
            pltpu.VMEM((pairs, 9) + plane, F32),
            pltpu.VMEM((pairs, 3) + plane, F32),
            pltpu.VMEM((pairs, 3, half_rows, lanes), F32),
            pltpu.VMEM((2 * rows, 3 * rows), BF16),
            pltpu.VMEM((3 * rows, 4 * lanes), BF16),
            pltpu.VMEM((2 * rows, 4 * lanes), F32),
            pltpu.VMEM((2, half_rows, lanes), F32),
            pltpu.VMEM((2,) + plane, F32),
            pltpu.VMEM(plane, F32),
            pltpu.VMEM(plane, F32),
            pltpu.VMEM(plane, F32),
            pltpu.VMEM((2,) + plane, F32),
            pltpu.VMEM(plane, F32),
            pltpu.VMEM(plane, F32),
            dma((pairs,)), dma((pairs,)),
            dma((4,)), dma((4,)),
            dma((4,)), dma((4,)),
            dma((pairs,)), dma((pairs,)),
        ],
        compiler_params=pltpu.CompilerParams(
            collective_id=0, has_side_effects=True, vmem_limit_bytes=56 * 1024 * 1024
        ),
        name="adjoint_steps",
    )(adjoint, base_flow, viscosity, first_matrix, second_matrix)


def solution(mesh):
    return jax.shard_map(
        per_device,
        mesh=mesh,
        in_specs=(
            P(None, "gx", "gy", "gz"),
            P(None, "gx", "gy", "gz"),
            P("gx", "gy", "gz"),
            P(),
            P(),
        ),
        out_specs=P(None, "gx", "gy", "gz"),
        check_vma=False,
    )
```

time: 391 us -> 151 us (0.39)
  waiting for transfers between devices: 252 us -> 0 us
  Pallas kernels: 0 us -> 147 us
  other arithmetic: 53.3 us -> 0 us
  local copies, waits for them, and re-layouts: 29.4 us -> 3.91 us
  matrix products: 23.9 us -> 0 us
  starting transfers between devices: 15.6 us -> 0 us
  between operations: 13.4 us -> 0.01 us
    all_gather x3 -> x0, waiting for transfers between devices: 184 us -> none  [the longest x2 184 us: normal_derivs(): lax.all_gather(extended, 'gy', axis=2, tiled=True)]
    pallas_call x0 -> x1, Pallas kernels: none -> 147 us  [per_device(): pl.pallas_call(kernel, out_shape=jax.ShapeDtypeStruct(adjoint.shape, F32)...]
    ppermute x12 -> x0, waiting for transfers between devices: 67.8 us -> none  [the longest x6 34.1 us: with_halo(): after = lax.ppermute(initial, axis, down)]
    mul x4 -> x0, other arithmetic: 35.2 us -> none  [the longest x2 29.3 us: advance_state(): return updated * wall_mask]
    dot_general x3 -> x0, matrix products: 23.9 us -> none  [the longest x2 19.1 us: normal_derivs(): jnp.einsum('kij,cxjz->kcxiz', owned, lax.all_gather(extended, 'gy', axis=...]
    concatenate x7 -> x0, other arithmetic: 18 us -> none  [the longest x6 16.5 us: with_halo(): shard = jnp.concatenate([before, shard, after], axis=dim)]
    ppermute x12 -> x0, starting transfers between devices: 15.3 us -> none  [the longest x6 8.82 us: with_halo(): before = lax.ppermute(last, axis, up)]
    mul x5 -> x0, local copies, waits for them, and re-layouts: 12.3 us -> none  [the longest x1 3.55 us: advance_state(): return updated * wall_mask]
  transfers between devices with their start and end apart: 15 -> 0, of which waited for: 14 -> 0; matrix products, arithmetic and copies ran while one was open for 9% -> 0% of each run, Pallas kernels for 0% -> 0%
where the time goes in v1:
time: 151 us
  Pallas kernels  147 us (97%)
  local copies, waits for them, and re-layouts  3.91 us (3%)
    pallas_call x1, Pallas kernels, per_device(): pl.pallas_call(kernel, out_shape=jax.ShapeDtypeStruct(adjoint.shape, F32)...  147 us
    unnamed x1, local copies, waits for them, and re-layouts  3.91 us

profile of v1, /device:TPU:3, one launch (start us, length us, event | category | flops | bytes accessed | tf_op | source)
XLA Modules:
  0.0 151.3 jit_solution(16568189248758061220)
XLA Ops:
  0.0 147.4 %adjoint_steps.1 = f32[3,16,128,128]{3,2,1,0:T(8,128)} custom-call(f32[3,16,128,128]{3,2,1,0:T(8,128)} %adj.1, f32[3,16,128,128]{3,2,1,0:T(8,128)} %flow.1, f32[16,128,128]{2,1,0:T(8,128)} %visc.1, f32[256,256]{1,0:T(8,128)} %first_m.1, f32[256,256]{1,0:T(8,128)} %second_m.1), custom_call_target="tpu_custom_call" | custom-call | tf_op jit(solution)/shard_map/adjoint_steps/pallas_call | solution.py:307
  147.4 3.9 %copy.7 = f32[3,16,128,128]{3,2,1,0:T(8,128)} copy(f32[3,16,128,128]{3,2,1,0:T(8,128)} %adjoint_steps.1) | data formatting | bytes 6291456

commit v2 on v1

--- a/solution.py
+++ b/solution.py
@@ -12,16 +12,18 @@
 
 
 def kernel(
-    adj, flow, visc, first_m, second_m, out,
+    adj_in, flow_in, visc_in, first_m, second_m, out_hbm,
+    adj, flow, visc, out,
     send, state, mid, coef, late, back, matrix, rhs, derived,
-    edge_out, edges, outer, rim_lo, rim_hi, edges1, inner1, outer1,
-    swap_s, swap_r, edge_s, edge_r, rim_s, rim_r, ret_s, ret_r,
+    edge_out, edges, outer, rim_lo, rim_hi, edges1, inner1, outer1, rim1_lo, rim1_hi,
+    swap_s, swap_r, edge_s, edge_r, rim_s, rim_r, ret_s, ret_r, load_s, store_s,
 ):
-    _, cells, half_rows, lanes = adj.shape
+    _, cells, half_rows, lanes = adj_in.shape
     rows = 2 * half_rows
     half = lanes // 2
     pairs = cells // 2
     chunk = 32
+    early = pairs * 3 // 8
     ngx, ngz = lax.axis_size("gx"), lax.axis_size("gz")
     gy, gx, gz = lax.axis_index("gy"), lax.axis_index("gx"), lax.axis_index("gz")
     upper = lax.rem(gy + gz, 2)
@@ -45,8 +47,33 @@
 
     swap_edges = remote(edge_out, edges.at[:, mine, :], edge_s.at[0], edge_r.at[0], peer)
     pass_edge = remote(edges.at[1], outer, edge_s.at[1], edge_r.at[1], beside)
-    swap_inner1 = remote(edges1.at[0], inner1, edge_s.at[2], edge_r.at[2], peer)
-    pass_outer1 = remote(edges1.at[1], outer1, edge_s.at[3], edge_r.at[3], beside)
+
+    def edge_copies(g):
+        s, r = edge_s.at[2 + 2 * g], edge_r.at[2 + 2 * g]
+        inner = remote(edges1.at[g, 0], inner1.at[g], s, r, peer)
+        s, r = edge_s.at[3 + 2 * g], edge_r.at[3 + 2 * g]
+        return inner, remote(edges1.at[g, 1], outer1.at[g], s, r, beside)
+
+    def loads(p):
+        cells_of = pl.ds(2 * p, 2)
+        return (
+            pltpu.make_async_copy(adj_in.at[:, cells_of], adj.at[:, cells_of], load_s.at[0, p]),
+            pltpu.make_async_copy(visc_in.at[cells_of], visc.at[cells_of], load_s.at[1, p]),
+            pltpu.make_async_copy(flow_in.at[:, cells_of], flow.at[:, cells_of], load_s.at[2, p]),
+        )
+
+    def store(p):
+        cells_of = pl.ds(2 * p, 2)
+        return pltpu.make_async_copy(out.at[:, cells_of], out_hbm.at[:, cells_of], store_s.at[p])
+
+    for copy in loads(0):
+        copy.start()
+
+    @pl.loop(1, pairs)
+    def _(i):
+        for copy in loads(pairs - i):
+            copy.start()
+
     rim_left0 = remote(
         state.at[1, 0:4], state.at[pairs + 1, 0:4], rim_s.at[0], rim_r.at[0], left
     )
@@ -68,6 +95,8 @@
         return pltpu.roll(values, lax.rem(shift + 2 * lanes, lanes), 1)
 
     def pack(p):
+        for copy in loads(p):
+            copy.wait()
         for f in range(7):
             if f < 3:
                 even, odd = adj[f, 2 * p], adj[f, 2 * p + 1]
@@ -109,10 +138,7 @@
 
     swap_edges.start()
     swap(pairs - 2).start()
-
-    @pl.loop(1, pairs - 2)
-    def _(p):
-        swap(p).start()
+    swap(1).start()
 
     for s, source in enumerate((first_m, second_m)):
         values = source[...]
@@ -144,18 +170,29 @@
     in_half = lax.rem(clane, half)
     cslot = lax.rem(clane, half) // 2
 
-    def join_rims(inner, outside):
+    def join_rims():
         choose = jnp.full((rows, lanes), upper, jnp.int32) == 1
-        rim_lo[...] = jnp.where(choose, inner, outside)
-        rim_hi[...] = jnp.where(choose, outside, inner)
+        rim_lo[...] = jnp.where(choose, edges[0], outer[...])
+        rim_hi[...] = jnp.where(choose, outer[...], edges[0])
+
+    def join_rims1(g):
+        rim1_lo[g] = jnp.where(is_upper, inner1[g], outer1[g])
+        rim1_hi[g] = jnp.where(is_upper, outer1[g], inner1[g])
+
+    def rim1_place(p, c, r):
+        g = jnp.where(p < early, 0, 1)
+        count = jnp.where(p < early, early, pairs - early)
+        h = r * chunk // half_rows
+        k = c * count + p - g * early + h * (3 * count)
+        return g, k, pl.ds(pl.multiple_of(r * chunk - h * half_rows, chunk), chunk)
 
     def x_views(current, before, after):
         east = pltpu.roll(jnp.where(lower_lanes, after, current), half, 1)
         west = pltpu.roll(jnp.where(lower_lanes, current, before), half, 1)
         return east, west
 
-    def z_rims(k, at):
-        return turn(rim_lo[at, :], lanes - 2 - 2 * k), turn(rim_hi[at, :], half - 2 * k)
+    def z_rims(low, high, k):
+        return turn(low, lanes - 2 - 2 * k), turn(high, half - 2 * k)
 
     def z_views(current, rims, step):
         under = jnp.where(in_half >= half - step, rims[0], current)
@@ -168,14 +205,16 @@
             at = pl.ds(pl.multiple_of(r * chunk, chunk), chunk)
             centre = state[p + 1, 3, at, :]
             east, west = x_views(centre, state[p, 3, at, :], state[p + 2, 3, at, :])
-            lower, above = z_views(centre, z_rims(3 * pairs + p, at), 1)
+            lower, above = z_views(
+                centre, z_rims(rim_lo[at, :], rim_hi[at, :], 3 * pairs + p), 1
+            )
             ve, vw = 0.05 * (centre + east), 0.05 * (centre + west)
             vu, vl = 0.05 * (centre + above), 0.05 * (centre + lower)
             bx, by, bz = state[p + 1, 4, at, :], state[p + 1, 5, at, :], state[p + 1, 6, at, :]
             bx6, bz6 = bx * (1.0 / 6.0), bz * (1.0 / 6.0)
             coef[p, 0, at, :] = 1.0 - (ve + vw) - (vu + vl)
-            coef[p, 1, at, :] = bx6 + ve
-            coef[p, 2, at, :] = vw - bx6
+            coef[p, 1, at, :] = pltpu.roll(bx6 + ve, half, 1)
+            coef[p, 2, at, :] = pltpu.roll(vw - bx6, half, 1)
             coef[p, 3, at, :] = bx * (1.0 / 48.0)
             coef[p, 4, at, :] = bz6 + vu
             coef[p, 5, at, :] = vl - bz6
@@ -183,7 +222,7 @@
             coef[p, 7, at, :] = 0.25 * by + 0.1 * derived[at, 3 * lanes : 4 * lanes]
             coef[p, 8, at, :] = 0.1 * centre
 
-    def advance(source, p, target, place, with_edges):
+    def advance(source, p, target, place, is_first):
         @pl.loop(0, rows // chunk)
         def _(r):
             at = pl.ds(pl.multiple_of(r * chunk, chunk), chunk)
@@ -192,18 +231,25 @@
             inside = (row > 0) & (row < rows - 1)
             cs = [coef[p, n, at, :] for n in range(9)]
             for c in range(3):
-                k = c * pairs + p
+                g, k1, at1 = rim1_place(p, c, r)
                 current = source[p + 1, c, at, :]
                 before, after = source[p, c, at, :], source[p + 2, c, at, :]
-                east, west = x_views(current, before, after)
-                rims = z_rims(k, at)
+                beside_x = pltpu.roll(
+                    cs[1] * jnp.where(lower_lanes, after, current)
+                    + cs[2] * jnp.where(lower_lanes, current, before),
+                    half,
+                    1,
+                )
+                if is_first:
+                    rims = z_rims(rim_lo[at, :], rim_hi[at, :], c * pairs + p)
+                else:
+                    rims = z_rims(rim1_lo[g, at1, :], rim1_hi[g, at1, :], k1)
                 lower, above = z_views(current, rims, 1)
                 lower2, above2 = z_views(current, rims, 2)
                 columns = slice(c * lanes, (c + 1) * lanes)
                 value = (
                     cs[0] * current
-                    + cs[1] * east
-                    + cs[2] * west
+                    + beside_x
                     + cs[3] * (before - after)
                     + cs[4] * above
                     + cs[5] * lower
@@ -213,14 +259,17 @@
                 )
                 value = jnp.where(inside, value, 0.0)
                 target[place, c, at, :] = value
-                if with_edges:
-                    slot = cslot == k
-                    edges1[0, at, :] = jnp.where(
-                        slot, turn(value, 2 * k + far * (1 - upper)), edges1[0, at, :]
-                    )
-                    edges1[1, at, :] = jnp.where(
-                        slot, turn(value, 2 * k + far * upper), edges1[1, at, :]
-                    )
+                if is_first:
+                    slot = cslot == k1
+                    for e, shift in ((0, far * (1 - upper)), (1, far * upper)):
+                        edges1[g, e, at1, :] = jnp.where(
+                            slot, turn(value, 2 * k1 + shift), edges1[g, e, at1, :]
+                        )
+
+    def second_step(p):
+        split(mid, p + 1, 3)
+        advance(mid, p, late, p, False)
+        give_back(p).start()
 
     swap(0).wait_recv()
     rim_left0.start()
@@ -229,7 +278,7 @@
     swap_edges.wait_recv()
     pass_edge.start()
     pass_edge.wait_recv()
-    join_rims(edges[0], outer[...])
+    join_rims()
 
     @pl.loop(0, pairs)
     def _(i):
@@ -249,6 +298,10 @@
         def _():
             swap(i).wait_recv()
 
+        @pl.when(i < early)
+        def _():
+            swap(i + 2).start()
+
         split(state, p + 1, 4)
         coefficients(p)
         advance(state, p, mid, p + 1, True)
@@ -261,19 +314,33 @@
         def _():
             rim_left1.start()
 
-    swap_inner1.start()
-    pass_outer1.start()
-    swap_inner1.wait_recv()
-    pass_outer1.wait_recv()
+        @pl.when(i == early)
+        def _():
+            for copy in edge_copies(0):
+                copy.start()
+            swap(pairs - 3).start()
+
+        @pl.when(i == early + 1)
+        def _():
+            for copy in edge_copies(0):
+                copy.wait_recv()
+            join_rims1(0)
+            rim_right1.wait_recv()
+
+            @pl.loop(0, early)
+            def _(q):
+                second_step(q)
+
+    for copy in edge_copies(1):
+        copy.start()
+    for copy in edge_copies(1):
+        copy.wait_recv()
+    join_rims1(1)
     rim_left1.wait_recv()
-    rim_right1.wait_recv()
-    join_rims(inner1[...], outer1[...])
-
-    @pl.loop(0, pairs)
+
+    @pl.loop(early, pairs)
     def _(p):
-        split(mid, p + 1, 3)
-        advance(mid, p, late, p, False)
-        give_back(p).start()
+        second_step(p)
 
     @pl.loop(0, pairs)
     def _(p):
@@ -285,14 +352,16 @@
             highs = jnp.where(is_upper, keep, got)
             out[c, 2 * p] = jnp.where(lane < half, lows, pltpu.roll(highs, half, 1))
             out[c, 2 * p + 1] = jnp.where(lane < half, pltpu.roll(lows, half, 1), highs)
+        store(p).start()
 
     @pl.loop(0, pairs)
     def _(p):
         swap(p).wait_send()
         give_back(p).wait_send()
+        store(p).wait()
 
     for copy in (
-        swap_edges, pass_edge, swap_inner1, pass_outer1,
+        swap_edges, pass_edge, *edge_copies(0), *edge_copies(1),
         rim_left0, rim_right0, rim_left1, rim_right1,
     ):
         copy.wait_send()
@@ -303,13 +372,18 @@
     rows, pairs = 2 * half_rows, cells // 2
     plane = (rows, lanes)
     vmem = pl.BlockSpec(memory_space=pltpu.VMEM)
+    anywhere = pl.BlockSpec(memory_space=pl.ANY)
     dma = pltpu.SemaphoreType.DMA
     return pl.pallas_call(
         kernel,
         out_shape=jax.ShapeDtypeStruct(adjoint.shape, F32),
-        in_specs=[vmem] * 5,
-        out_specs=vmem,
+        in_specs=[anywhere] * 3 + [vmem] * 2,
+        out_specs=anywhere,
         scratch_shapes=[
+            pltpu.VMEM(adjoint.shape, F32),
+            pltpu.VMEM(base_flow.shape, F32),
+            pltpu.VMEM(viscosity.shape, F32),
+            pltpu.VMEM(adjoint.shape, F32),
             pltpu.VMEM((pairs, 7, half_rows, lanes), F32),
             pltpu.VMEM((pairs + 2, 7) + plane, F32),
             pltpu.VMEM((pairs + 2, 3) + plane, F32),
@@ -324,13 +398,16 @@
             pltpu.VMEM(plane, F32),
             pltpu.VMEM(plane, F32),
             pltpu.VMEM(plane, F32),
-            pltpu.VMEM((2,) + plane, F32),
-            pltpu.VMEM(plane, F32),
-            pltpu.VMEM(plane, F32),
+            pltpu.VMEM((2, 2, half_rows, lanes), F32),
+            pltpu.VMEM((2, half_rows, lanes), F32),
+            pltpu.VMEM((2, half_rows, lanes), F32),
+            pltpu.VMEM((2, half_rows, lanes), F32),
+            pltpu.VMEM((2, half_rows, lanes), F32),
             dma((pairs,)), dma((pairs,)),
-            dma((4,)), dma((4,)),
+            dma((6,)), dma((6,)),
             dma((4,)), dma((4,)),
             dma((pairs,)), dma((pairs,)),
+            dma((3, pairs)), dma((pairs,)),
         ],
         compiler_params=pltpu.CompilerParams(
             collective_id=0, has_side_effects=True, vmem_limit_bytes=56 * 1024 * 1024

time: 151 us -> 138 us (0.914)
  Pallas kernels: 147 us -> 134 us
    pallas_call x1, Pallas kernels: 147 us -> 134 us  [per_device(): pl.pallas_call(kernel, out_shape=jax.ShapeDtypeStruct(adjoint.shape, F32)...]
where the time goes in v2:
time: 138 us
  Pallas kernels  134 us (97%)
  local copies, waits for them, and re-layouts  3.91 us (3%)
    pallas_call x1, Pallas kernels, per_device(): pl.pallas_call(kernel, out_shape=jax.ShapeDtypeStruct(adjoint.shape, F32)...  134 us
    unnamed x1, local copies, waits for them, and re-layouts  3.91 us

profile of v2, /device:TPU:3, one launch (start us, length us, event | category | flops | bytes accessed | tf_op | source)
XLA Modules:
  0.0 137.6 jit_solution(7832312499376609187)
XLA Ops:
  0.0 133.7 %adjoint_steps.1 = f32[3,16,128,128]{3,2,1,0:T(8,128)} custom-call(f32[3,16,128,128]{3,2,1,0:T(8,128)} %adj_in.1, f32[3,16,128,128]{3,2,1,0:T(8,128)} %flow_in.1, f32[16,128,128]{2,1,0:T(8,128)} %visc_in.1, f32[256,256]{1,0:T(8,128)} %first_m.1, f32[256,256]{1,0:T(8,128)} %second_m.1), custom_call_target="tpu_custom_call" | custom-call | tf_op jit(solution)/shard_map/adjoint_steps/pallas_call | solution.py:377
  133.7 3.9 %copy.7 = f32[3,16,128,128]{3,2,1,0:T(8,128)} copy(f32[3,16,128,128]{3,2,1,0:T(8,128)} %adjoint_steps.1) | data formatting | bytes 6291456

commit v3 on v2

--- a/solution.py
+++ b/solution.py
@@ -367,6 +367,18 @@
         copy.wait_send()
 
 
+def hand_over(source, target, sems):
+    cells = source.shape[1]
+
+    def copy(x):
+        return pltpu.make_async_copy(source.at[:, x], target.at[:, x], sems.at[x])
+
+    for x in range(cells):
+        copy(x).start()
+    for x in range(cells):
+        copy(x).wait()
+
+
 def per_device(adjoint, base_flow, viscosity, first_matrix, second_matrix):
     _, cells, half_rows, lanes = adjoint.shape
     rows, pairs = 2 * half_rows, cells // 2
@@ -374,7 +386,7 @@
     vmem = pl.BlockSpec(memory_space=pltpu.VMEM)
     anywhere = pl.BlockSpec(memory_space=pl.ANY)
     dma = pltpu.SemaphoreType.DMA
-    return pl.pallas_call(
+    result = pl.pallas_call(
         kernel,
         out_shape=jax.ShapeDtypeStruct(adjoint.shape, F32),
         in_specs=[anywhere] * 3 + [vmem] * 2,
@@ -414,6 +426,15 @@
         ),
         name="adjoint_steps",
     )(adjoint, base_flow, viscosity, first_matrix, second_matrix)
+    return pl.pallas_call(
+        hand_over,
+        out_shape=jax.ShapeDtypeStruct(adjoint.shape, F32),
+        in_specs=[anywhere],
+        out_specs=anywhere,
+        scratch_shapes=[dma((cells,))],
+        compiler_params=pltpu.CompilerParams(vmem_limit_bytes=62 * 1024 * 1024),
+        name="hand_over",
+    )(result)
 
 
 def solution(mesh):

time: 138 us -> 230 us (1.67)
  Pallas kernels: 134 us -> 230 us
  local copies, waits for them, and re-layouts: 3.91 us -> 0 us
    pallas_call x0 -> x1, Pallas kernels: none -> 96.5 us  [per_device(): pl.pallas_call(hand_over, out_shape=jax.ShapeDtypeStruct(adjoint.shape, F...]
    unnamed x1 -> x0, local copies, waits for them, and re-layouts: 3.91 us -> none
where the time goes in v3:
time: 230 us
  Pallas kernels  230 us (100%)
    pallas_call x1, Pallas kernels, per_device(): pl.pallas_call(kernel, out_shape=jax.ShapeDtypeStruct(adjoint.shape, F32)...  134 us
    pallas_call x1, Pallas kernels, per_device(): pl.pallas_call(hand_over, out_shape=jax.ShapeDtypeStruct(adjoint.shape, F...  96.5 us

profile of v3, /device:TPU:3, one launch (start us, length us, event | category | flops | bytes accessed | tf_op | source)
XLA Modules:
  0.0 230.2 jit_solution(4484080414105372658)
XLA Ops:
  0.0 133.7 %adjoint_steps.1.source = f32[3,16,128,128]{3,2,1,0:T(8,128)} custom-call(f32[3,16,128,128]{3,2,1,0:T(8,128)} %adj_in.1, f32[3,16,128,128]{3,2,1,0:T(8,128)} %flow_in.1, f32[16,128,128]{2,1,0:T(8,128)} %visc_in.1, f32[256,256]{1,0:T(8,128)} %first_m.1, f32[256,256]{1,0:T(8,128)} %second_m.1), custom_call_target="tpu_custom_call" | custom-call | tf_op jit(solution)/shard_map/adjoint_steps/pallas_call | solution.py:389
  133.7 96.5 %hand_over.1 = f32[3,16,128,128]{3,2,1,0:T(8,128)} custom-call(f32[3,16,128,128]{3,2,1,0:T(8,128)} %adjoint_steps.1.source), custom_call_target="tpu_custom_call" | custom-call | tf_op jit(solution)/shard_map/hand_over/pallas_call | solution.py:429

commit v4 on v2

--- a/solution.py
+++ b/solution.py
@@ -367,6 +367,10 @@
         copy.wait_send()
 
 
+def hand_over(source, target):
+    target[...] = source[...]
+
+
 def per_device(adjoint, base_flow, viscosity, first_matrix, second_matrix):
     _, cells, half_rows, lanes = adjoint.shape
     rows, pairs = 2 * half_rows, cells // 2
@@ -374,7 +378,7 @@
     vmem = pl.BlockSpec(memory_space=pltpu.VMEM)
     anywhere = pl.BlockSpec(memory_space=pl.ANY)
     dma = pltpu.SemaphoreType.DMA
-    return pl.pallas_call(
+    result = pl.pallas_call(
         kernel,
         out_shape=jax.ShapeDtypeStruct(adjoint.shape, F32),
         in_specs=[anywhere] * 3 + [vmem] * 2,
@@ -414,6 +418,16 @@
         ),
         name="adjoint_steps",
     )(adjoint, base_flow, viscosity, first_matrix, second_matrix)
+    block = pl.BlockSpec((3, 4, half_rows, lanes), lambda x: (0, x, 0, 0))
+    return pl.pallas_call(
+        hand_over,
+        out_shape=jax.ShapeDtypeStruct(adjoint.shape, F32),
+        grid=(cells // 4,),
+        in_specs=[block],
+        out_specs=block,
+        compiler_params=pltpu.CompilerParams(vmem_limit_bytes=62 * 1024 * 1024),
+        name="hand_over",
+    )(result)
 
 
 def solution(mesh):

time: 138 us -> 138 us (level)
  Pallas kernels: 134 us -> 138 us
  local copies, waits for them, and re-layouts: 3.91 us -> 0 us
    pallas_call x0 -> x1, Pallas kernels: none -> 4.2 us  [per_device(): pl.pallas_call(hand_over, out_shape=jax.ShapeDtypeStruct(adjoint.shape, F...]
    unnamed x1 -> x0, local copies, waits for them, and re-layouts: 3.91 us -> none
where the time goes in v4:
time: 138 us
  Pallas kernels  138 us (100%)
    pallas_call x1, Pallas kernels, per_device(): pl.pallas_call(kernel, out_shape=jax.ShapeDtypeStruct(adjoint.shape, F32)...  134 us
    pallas_call x1, Pallas kernels, per_device(): pl.pallas_call(hand_over, out_shape=jax.ShapeDtypeStruct(adjoint.shape, F...  4.2 us

profile of v4, /device:TPU:3, one launch (start us, length us, event | category | flops | bytes accessed | tf_op | source)
XLA Modules:
  0.0 137.9 jit_solution(13002025478598517834)
XLA Ops:
  0.0 133.7 %adjoint_steps.1.source = f32[3,16,128,128]{3,2,1,0:T(8,128)} custom-call(f32[3,16,128,128]{3,2,1,0:T(8,128)} %adj_in.1, f32[3,16,128,128]{3,2,1,0:T(8,128)} %flow_in.1, f32[16,128,128]{2,1,0:T(8,128)} %visc_in.1, f32[256,256]{1,0:T(8,128)} %first_m.1, f32[256,256]{1,0:T(8,128)} %second_m.1), custom_call_target="tpu_custom_call" | custom-call | tf_op jit(solution)/shard_map/adjoint_steps/pallas_call | solution.py:381
  133.7 4.2 %hand_over.1 = f32[3,16,128,128]{3,2,1,0:T(8,128)} custom-call(f32[3,16,128,128]{3,2,1,0:T(8,128)} %adjoint_steps.1.source), custom_call_target="tpu_custom_call" | custom-call | tf_op jit(solution)/shard_map/hand_over/pallas_call | solution.py:422
